TPU v7x, 32 devices: a whole 2x2x4 slice. The times are simulated.
32 devices in a mesh: band: 4 (over y, core), grid: 8 (over z, x).
Axes of the slice: x: 2, y: 2, z: 4, core: 2. Of those that a mesh axis runs over, the one named last changes fastest.
Arguments:
- ground: float32 [4, 128, 128, 128], P('band', 'grid'), may hold values from -6 to 6
- response: float32 [4, 2, 2, 128, 128, 128], P('band', None, None, None, 'grid'), may hold values from -0.6 to 0.6
- kernel_xc: float32 [128, 128, 128], P('grid'), may hold values from -2 to -0.3
Outputs:
- applied: float32 [4, 2, 2, 128, 128, 128], P('band', None, None, None, 'grid')
All inputs are finite; a program needn't handle non-finite values.
Results may differ from a plain program's by a relative error of at most 0.0001.
Values sent between devices are 32-bit elements; how exact they have to be, the bound alone decides.
A program may use at most 64 MiB of HBM per device.

v0:
```python
import math
import jax
import jax.numpy as jnp
import numpy as np
from jax import lax
from jax.sharding import PartitionSpec as P

high = lax.Precision.HIGH
spacing = 0.4527


def dft_pair(length, direction, rows=None, columns=None):
    rows = np.arange(length) if rows is None else rows
    columns = np.arange(length) if columns is None else columns
    angles = rows[:, None] * columns[None, :] % length * (2.0 * math.pi / length)
    cosine = np.cos(angles) / math.sqrt(length)
    sine = direction * np.sin(angles) / math.sqrt(length)
    pairs = (np.stack((cosine, sine), axis=1), np.stack((-sine, cosine), axis=1))
    return np.stack(pairs, axis=0).astype(np.float32)


def ein(form, operand, table):
    return jnp.einsum(form, operand, table, precision=high)


def signed_freq(positions, length):
    return jnp.where(positions < (length + 1) // 2, positions, positions - length).astype(
        jnp.float32
    )


def coulomb(freq_first, freq_second, freq_third, length):
    squares = (
        freq_first[:, None, None] ** 2
        + freq_second[None, :, None] ** 2
        + freq_third[None, None, :] ** 2
    )
    edge_len = spacing * length
    return jnp.where(
        squares > 0.5, edge_len * edge_len / (math.pi * jnp.maximum(squares, 1.0)), 0.0
    )


def swap(values, bit, size):
    return lax.ppermute(values, "band", [(i, i ^ bit) for i in range(size)])


def hartree(density, axes, device, devices, numbers):
    length = density.shape[-1]
    forward, backward = (dft_pair(length, -1.0), dft_pair(length, 1.0))
    wave = ein("cxyz,cydk->dxkz", density, forward)
    wave = ein("dxkz,dzem->exkm", wave, forward)
    wave = lax.all_to_all(wave, axes, split_axis=2, concat_axis=1, tiled=True)
    rows = length // devices
    mine = device * rows + jnp.arange(rows, dtype=jnp.int32)
    freqs = signed_freq(jnp.arange(length, dtype=jnp.int32), length)
    weights = coulomb(freqs, signed_freq(mine, length), freqs, length)
    wave = ein("cxyz,cxdk->dkyz", wave, dft_pair(length, -1.0, rows=numbers)) * weights
    wave = ein("dkyz,dkex->exyz", wave, dft_pair(length, 1.0, columns=numbers))
    wave = lax.all_to_all(wave, axes, split_axis=1, concat_axis=2, tiled=True)
    cell = ein("dxkz,dzem->exkm", wave, backward)
    return ein("cxyz,cydk->dxkz", cell, backward)


def on_device(bands, grids, ground, response, kernel_xc):
    grid_len = ground.shape[2]
    planes = ground.shape[1]
    forward = dft_pair(grid_len, -1.0)
    backward = dft_pair(grid_len, 1.0)
    orbital = ground[0]
    flip = np.array([1.0, -1.0], np.float32)[None, None, :, None]
    partial = None
    for harmonic in range(2):
        table = backward if harmonic == 0 else backward * flip
        wave = ein("cxyz,cxdk->dkyz", response[0, harmonic], backward)
        wave = lax.all_to_all(wave, "grid", split_axis=1, concat_axis=2, tiled=True)
        wave = ein("dxkz,dzem->exkm", wave, backward)
        cell = ein("cxyz,cydk->dxkz", wave, table)
        partial = cell if partial is None else partial + cell
    partial = partial * orbital
    me_band = lax.axis_index("band")
    if planes % bands == 0 and bands & bands - 1 == 0:
        dens = partial
        kernel = kernel_xc
        bit = bands // 2
        bits = []
        while bit >= 1:
            bits.append(bit)
            bit //= 2
        steps = list(reversed(bits))
        low = jnp.int32(0)
        for bit in steps:
            half = dens.shape[1] // 2
            mine = me_band // bit % 2
            keep = lax.dynamic_slice_in_dim(dens, mine * half, half, 1)
            give = lax.dynamic_slice_in_dim(dens, (1 - mine) * half, half, 1)
            dens = keep + swap(give, bit, bands)
            low = low + mine * half
        own = dens.shape[1]
        kernel = lax.dynamic_slice_in_dim(kernel_xc, low, own, 0)
        place = [0] * bands
        for b in range(bands):
            size = planes
            for bit in steps:
                size //= 2
                place[b] += b // bit % 2 * (size // own)
        numbers = (
            np.arange(grids)[None, :, None] * planes
            + np.array(place)[:, None, None] * own
            + np.arange(own)[None, None, :]
        ).reshape(-1)
        device = me_band * grids + lax.axis_index("grid")
        pot = hartree(dens, ("band", "grid"), device, bands * grids, numbers)
        pot = pot + kernel * dens
        for bit in reversed(steps):
            mine = me_band // bit % 2
            other = swap(pot, bit, bands)
            first = jnp.where(mine == 0, pot, other)
            second = jnp.where(mine == 0, other, pot)
            pot = jnp.concatenate((first, second), axis=1)
    else:
        dens = lax.psum(partial, "band")
        pot = hartree(dens, "grid", lax.axis_index("grid"), grids, None)
        pot = pot + kernel_xc * dens
    prod = pot * orbital
    outs = []
    for harmonic in range(2):
        table = forward if harmonic == 0 else forward * flip.reshape(2, 1, 1, 1)
        wave = ein("cxyz,cydk->dxkz", prod, table)
        wave = ein("dxkz,dzem->exkm", wave, forward)
        wave = lax.all_to_all(wave, "grid", split_axis=2, concat_axis=1, tiled=True)
        outs.append(ein("cxyz,cxdk->dkyz", wave, forward))
    return jnp.stack(outs, axis=0)[None]


def solution(mesh):
    bands, grids = (mesh.shape["band"], mesh.shape["grid"])

    def body(ground, response, kernel_xc):
        return on_device(bands, grids, ground, response, kernel_xc)

    return jax.shard_map(
        body,
        mesh=mesh,
        in_specs=(
            P("band", "grid", None, None),
            P("band", None, None, None, "grid", None),
            P("grid", None, None),
        ),
        out_specs=P("band", None, None, None, "grid", None),
        check_vma=False,
    )
```

profile of v0, /device:TPU:0, one launch (start us, length us, event | category | flops | bytes accessed | tf_op | source)
XLA Modules:
  0.0 335.6 jit_solution(17473547233296567763)
XLA Ops:
  0.0 4.0 %fusion.46 = (f32[1,1,2,128,16,128]{5,4,3,2,1,0:T(8,128)S(1)}, f32[1,1,2,128,16,128]{5,4,3,2,1,0:T(8,128)}) fusion(f32[1,2,2,128,16,128]{5,4,3,2,1,0:T(8,128)} %param.22), kind=kLoop, calls=%fused_computation.68 | loop fusion | bytes 8388608 | tf_op jit(solution)/shard_map/slice | solution.py:75
  5.7 2.5 copy.81
  8.2 7.3 %all-to-all-start = ((f32[2,128,16,128]{3,2,0,1:T(8,128)}), f32[2,128,16,128]{3,2,0,1:T(8,128)}, u32[]{:S(2)}, u32[]{:S(2)}) async-start(f32[2,128,16,128]{3,2,0,1:T(8,128)} %copy.81), calls=%async_computation | async-start | bytes 4194304 | tf_op jit(solution)/shard_map/all_to_all | solution.py:76
  15.5 3.2 fusion.24
  18.6 2.5 copy.89
  21.2 42.6 %all-to-all-done = f32[2,128,16,128]{3,2,0,1:T(8,128)} async-done(((f32[2,128,16,128]{3,2,0,1:T(8,128)}), f32[2,128,16,128]{3,2,0,1:T(8,128)}, u32[]{:S(2)}, u32[]{:S(2)}) %all-to-all-start) | async-done | bytes 2097184 | tf_op jit(solution)/shard_map/all_to_all | solution.py:76
  63.8 4.5 %all-to-all-start.1 = ((f32[2,128,16,128]{3,2,0,1:T(8,128)}), f32[2,128,16,128]{3,2,0,1:T(8,128)}, u32[]{:S(2)}, u32[]{:S(2)}) async-start(f32[2,128,16,128]{3,2,0,1:T(8,128)} %copy.89), calls=%async_computation.1 | async-start | bytes 4194304 | tf_op jit(solution)/shard_map/all_to_all | solution.py:76
  68.7 3.2 copy.83
  72.0 44.1 %all-to-all-done.1 = f32[2,128,16,128]{3,2,0,1:T(8,128)} async-done(((f32[2,128,16,128]{3,2,0,1:T(8,128)}), f32[2,128,16,128]{3,2,0,1:T(8,128)}, u32[]{:S(2)}, u32[]{:S(2)}) %all-to-all-start.1) | async-done | bytes 2097184 | tf_op jit(solution)/shard_map/all_to_all | solution.py:76
  125.7 2.7 collective-permute-done
  132.5 12.8 %collective-permute-done.1 = f32[2,4,128,128]{2,3,0,1:T(8,128)} collective-permute-done((f32[2,4,128,128]{2,3,0,1:T(8,128)}, f32[2,4,128,128]{2,3,0,1:T(8,128)}, u32[]{:S(2)}, u32[]{:S(2)}) %collective-permute-start.1) | collective-permute-done | bytes 524320 | tf_op jit(solution)/shard_map/ppermute | solution.py:45
  148.5 3.7 %all-to-all-start.2 = ((f32[2,4,128,128]{3,0,1,2:T(2,128)}), f32[2,4,128,128]{3,0,1,2:T(2,128)}, u32[]{:S(2)}, u32[]{:S(2)}) async-start(f32[2,4,128,128]{3,0,1,2:T(2,128)} %copy.97), calls=%async_computation.2 | async-start | bytes 1048576 | tf_op jit(solution)/shard_map/all_to_all | solution.py:53
  153.2 15.4 %all-to-all-done.2 = f32[2,4,128,128]{3,0,1,2:T(2,128)} async-done(((f32[2,4,128,128]{3,0,1,2:T(2,128)}), f32[2,4,128,128]{3,0,1,2:T(2,128)}, u32[]{:S(2)}, u32[]{:S(2)}) %all-to-all-start.2) | async-done | bytes 524320 | tf_op jit(solution)/shard_map/all_to_all | solution.py:53
  172.7 3.6 %all-to-all-start.3 = ((f32[2,128,4,128]{3,2,0,1:T(4,128)}), f32[2,128,4,128]{3,2,0,1:T(4,128)}, u32[]{:S(2)}, u32[]{:S(2)}) async-start(f32[2,128,4,128]{3,2,0,1:T(4,128)} %copy.100), calls=%async_computation.3 | async-start | bytes 1048576 | tf_op jit(solution)/shard_map/all_to_all | solution.py:60
  178.2 14.2 %all-to-all-done.3 = f32[2,128,4,128]{3,2,0,1:T(4,128)} async-done(((f32[2,128,4,128]{3,2,0,1:T(4,128)}), f32[2,128,4,128]{3,2,0,1:T(4,128)}, u32[]{:S(2)}, u32[]{:S(2)}) %all-to-all-start.3) | async-done | bytes 524320 | tf_op jit(solution)/shard_map/all_to_all | solution.py:60
  197.4 12.5 %collective-permute-done.2 = f32[2,4,128,128]{2,3,0,1:T(8,128)S(1)} collective-permute-done((f32[2,4,128,128]{2,3,0,1:T(8,128)S(1)}, f32[2,4,128,128]{2,3,0,1:T(8,128)S(1)}, u32[]{:S(2)}, u32[]{:S(2)}) %collective-permute-start.2) | collective-permute-done | bytes 524320 | tf_op jit(solution)/shard_map/ppermute | solution.py:45
  218.6 2.9 copy.112
  221.5 4.3 %all-to-all-start.5 = ((f32[2,16,128,128]{3,0,1,2:T(2,128)}), f32[2,16,128,128]{3,0,1,2:T(2,128)}, u32[]{:S(2)}, u32[]{:S(2)}) async-start(f32[2,16,128,128]{3,0,1,2:T(2,128)} %copy.112), calls=%async_computation.5 | async-start | bytes 4194304 | tf_op jit(solution)/shard_map/all_to_all | solution.py:131
  228.7 2.9 copy.108
  231.7 43.0 %all-to-all-done.5 = f32[2,16,128,128]{3,0,1,2:T(2,128)} async-done(((f32[2,16,128,128]{3,0,1,2:T(2,128)}), f32[2,16,128,128]{3,0,1,2:T(2,128)}, u32[]{:S(2)}, u32[]{:S(2)}) %all-to-all-start.5) | async-done | bytes 2097184 | tf_op jit(solution)/shard_map/all_to_all | solution.py:131
  274.7 3.9 %all-to-all-start.4 = ((f32[2,16,128,128]{3,0,1,2:T(2,128)}), f32[2,16,128,128]{3,0,1,2:T(2,128)S(1)}, u32[]{:S(2)}, u32[]{:S(2)}) async-start(f32[2,16,128,128]{3,0,1,2:T(2,128)} %copy.108), calls=%async_computation.4 | async-start | bytes 4194304 | tf_op jit(solution)/shard_map/all_to_all | solution.py:131
  278.5 3.2 copy.113
  281.7 45.1 %all-to-all-done.4 = f32[2,16,128,128]{3,0,1,2:T(2,128)S(1)} async-done(((f32[2,16,128,128]{3,0,1,2:T(2,128)}), f32[2,16,128,128]{3,0,1,2:T(2,128)S(1)}, u32[]{:S(2)}, u32[]{:S(2)}) %all-to-all-start.4) | async-done | bytes 2097184 | tf_op jit(solution)/shard_map/all_to_all | solution.py:131
  331.2 4.4 %copy.115 = f32[1,2,2,128,16,128]{5,4,3,2,1,0:T(8,128)} copy(f32[1,2,2,128,16,128]{5,3,4,2,1,0:T(8,128)S(1)} %maximum_bitcast_fusion) | data formatting | bytes 8388608 | tf_op jit(solution)/shard_map/broadcast_in_dim | solution.py:133
  (76 shorter events, 46.4 us)
Async XLA Ops:
  0.0 176.3 %copy-start = (f32[16,128,128]{2,1,0:T(8,128)S(1)}, f32[16,128,128]{2,1,0:T(8,128)}, u32[]{:S(2)}) copy-start(f32[16,128,128]{2,1,0:T(8,128)} %param.23) | copy-start | bytes 3145732
  0.0 4.0 %copy-start.12 = (f32[2,128,2,128,1]{1,3,0,4,2:T(8,128)S(1)}, f32[2,128,2,128,1]{1,3,0,4,2:T(8,128)}, u32[]{:S(2)}) copy-start(f32[2,128,2,128,1]{1,3,0,4,2:T(8,128)} %constant.98) | copy-start | bytes 786436
  8.2 55.6 %all-to-all-start = ((f32[2,128,16,128]{3,2,0,1:T(8,128)}), f32[2,128,16,128]{3,2,0,1:T(8,128)}, u32[]{:S(2)}, u32[]{:S(2)}) async-start(f32[2,128,16,128]{3,2,0,1:T(8,128)} %copy.81), calls=%async_computation | async-start | bytes 4194304 | tf_op jit(solution)/shard_map/all_to_all | solution.py:76
  21.2 47.2 %copy-start.13 = (f32[1,16,128,128]{3,2,1,0:T(8,128)S(1)}, f32[1,16,128,128]{3,2,1,0:T(8,128)}, u32[]{:S(2)}) copy-start(f32[1,16,128,128]{3,2,1,0:T(8,128)} %param.21) | copy-start | bytes 3145732
  63.8 52.3 %all-to-all-start.1 = ((f32[2,128,16,128]{3,2,0,1:T(8,128)}), f32[2,128,16,128]{3,2,0,1:T(8,128)}, u32[]{:S(2)}, u32[]{:S(2)}) async-start(f32[2,128,16,128]{3,2,0,1:T(8,128)} %copy.89), calls=%async_computation.1 | async-start | bytes 4194304 | tf_op jit(solution)/shard_map/all_to_all | solution.py:76
  116.1 2.2 copy-start.2
  116.1 2.2 copy-start.6
  119.3 1.1 copy-start.14
  124.2 1.3 copy-start.4
  125.6 2.9 collective-permute-start
  125.7 19.5 %copy-start.5 = (f32[2,128,2,128,1]{3,1,0,2,4:T(8,128)S(1)}, f32[2,128,2,128,1]{3,1,0,2,4:T(8,128)}, u32[]{:S(2)}) copy-start(f32[2,128,2,128,1]{3,1,0,2,4:T(8,128)} %constant.101) | copy-start | bytes 786436
  131.0 14.3 %collective-permute-start.1 = (f32[2,4,128,128]{2,3,0,1:T(8,128)}, f32[2,4,128,128]{2,3,0,1:T(8,128)}, u32[]{:S(2)}, u32[]{:S(2)}) collective-permute-start(f32[2,4,128,128]{2,3,0,1:T(8,128)} %constant_dynamic-slice_fusion.1), channel_id=1, source_target_pairs={{0,16},{8,24},{16,0},{24,8},{1,17},{9,25},{17,1},{25,9},{2,18},{10... | collective-permute-start | bytes 1572872 | tf_op jit(solution)/shard_map/ppermute | solution.py:45
  148.5 20.0 %all-to-all-start.2 = ((f32[2,4,128,128]{3,0,1,2:T(2,128)}), f32[2,4,128,128]{3,0,1,2:T(2,128)}, u32[]{:S(2)}, u32[]{:S(2)}) async-start(f32[2,4,128,128]{3,0,1,2:T(2,128)} %copy.97), calls=%async_computation.2 | async-start | bytes 1048576 | tf_op jit(solution)/shard_map/all_to_all | solution.py:53
  168.5 2.7 copy-start.16
  172.7 19.7 %all-to-all-start.3 = ((f32[2,128,4,128]{3,2,0,1:T(4,128)}), f32[2,128,4,128]{3,2,0,1:T(4,128)}, u32[]{:S(2)}, u32[]{:S(2)}) async-start(f32[2,128,4,128]{3,2,0,1:T(4,128)} %copy.100), calls=%async_computation.3 | async-start | bytes 1048576 | tf_op jit(solution)/shard_map/all_to_all | solution.py:60
  177.0 17.9 %copy-start.7 = (f32[2,128,2,128,1]{1,3,0,2,4:T(8,128)S(1)}, f32[2,128,2,128,1]{1,3,0,2,4:T(8,128)}, u32[]{:S(2)}) copy-start(f32[2,128,2,128,1]{1,3,0,2,4:T(8,128)} %constant.99) | copy-start | bytes 786436
  196.6 13.3 %collective-permute-start.2 = (f32[2,4,128,128]{2,3,0,1:T(8,128)S(1)}, f32[2,4,128,128]{2,3,0,1:T(8,128)S(1)}, u32[]{:S(2)}, u32[]{:S(2)}) collective-permute-start(f32[2,4,128,128]{2,3,0,1:T(8,128)S(1)} %multiply_add_fusion), channel_id=1, source_target_pairs={{0,16},{8,24},{16,0},{24,8},{1,17},{9,25},{17,1},{25,9},{2,18},{10... | collective-permute-start | bytes 1572872 | tf_op jit(solution)/shard_map/ppermute | solution.py:45
  211.1 2.9 collective-permute-start.3
  212.0 3.7 %copy-start.15 = (f32[2,128,2,128,1]{3,1,0,2,4:T(8,128)S(1)}, f32[2,128,2,128,1]{3,1,0,2,4:T(8,128)}, u32[]{:S(2)}) copy-start(f32[2,128,2,128,1]{3,1,0,2,4:T(8,128)} %constant.100) | copy-start | bytes 786436
  221.5 53.2 %all-to-all-start.5 = ((f32[2,16,128,128]{3,0,1,2:T(2,128)}), f32[2,16,128,128]{3,0,1,2:T(2,128)}, u32[]{:S(2)}, u32[]{:S(2)}) async-start(f32[2,16,128,128]{3,0,1,2:T(2,128)} %copy.112), calls=%async_computation.5 | async-start | bytes 4194304 | tf_op jit(solution)/shard_map/all_to_all | solution.py:131
  274.7 52.1 %all-to-all-start.4 = ((f32[2,16,128,128]{3,0,1,2:T(2,128)}), f32[2,16,128,128]{3,0,1,2:T(2,128)S(1)}, u32[]{:S(2)}, u32[]{:S(2)}) async-start(f32[2,16,128,128]{3,0,1,2:T(2,128)} %copy.108), calls=%async_computation.4 | async-start | bytes 4194304 | tf_op jit(solution)/shard_map/all_to_all | solution.py:131
  326.8 1.6 copy-start.3
  326.8 1.6 copy-start.11
  331.2 4.5 %copy-start.1 = (f32[16,128,128]{2,1,0:T(8,128)S(1)}, f32[16,128,128]{2,1,0:T(8,128)}, u32[]{:S(2)}) copy-start(f32[16,128,128]{2,1,0:T(8,128)} %param.23) | copy-start | bytes 3145732
  (3 other events, 2.5 us)
where the time goes:
time: 337 us; the launch traced here: 336 us
  waiting for transfers between devices  234 us (69%)
  local copies, waits for them, and re-layouts  39.8 us (12%)
  starting transfers between devices  29.5 us (9%)
  matrix products  25.6 us (8%)
  other arithmetic  5.86 us (2%)
    all_to_all x2, waiting for transfers between devices, on_device(): wave = lax.all_to_all(wave, 'grid', split_axis=2, concat_axis=1, tiled=True)  88.1 us
    all_to_all x2, waiting for transfers between devices, on_device(): wave = lax.all_to_all(wave, 'grid', split_axis=1, concat_axis=2, tiled=True)  86.7 us
    ppermute x4, waiting for transfers between devices, swap(): return lax.ppermute(values, 'band', [(i, i ^ bit) for i in range(size)])  29.9 us
    dot_general x18, matrix products, ein(): return jnp.einsum(form, operand, table, precision=high)  25.6 us
    all_to_all x1, waiting for transfers between devices, hartree(): wave = lax.all_to_all(wave, axes, split_axis=2, concat_axis=1, tiled=True)  15.4 us
    all_to_all x1, waiting for transfers between devices, hartree(): wave = lax.all_to_all(wave, axes, split_axis=1, concat_axis=2, tiled=True)  14.2 us
    all_to_all x2, starting transfers between devices, on_device(): wave = lax.all_to_all(wave, 'grid', split_axis=1, concat_axis=2, tiled=True)  11.8 us
    all_to_all x2, starting transfers between devices, on_device(): wave = lax.all_to_all(wave, 'grid', split_axis=2, concat_axis=1, tiled=True)  8.2 us
  transfers between devices with their start and end apart: 10, of which 10 were waited for; matrix products, arithmetic and copies ran while one was open for 6% of the time, Pallas kernels for 0%

commit v1 on v0

--- a/solution.py
+++ b/solution.py
@@ -1,3 +1,4 @@
+import functools
 import math
 import jax
 import jax.numpy as jnp
@@ -7,6 +8,30 @@
 
 high = lax.Precision.HIGH
 spacing = 0.4527
+
+
+def turn_meshes(my_data, a_name):
+    z_new = jax.lax.axis_size(a_name)
+    f_now = jax.lax.axis_index(a_name)
+    view_out, front = (z_new, f_now)
+    o_now = my_data.shape[2] // view_out
+    b_now = list(my_data.shape)
+    b_now[2] = o_now
+    base_arr = b_now[1]
+    b_now[1] = base_arr * view_out
+    known = jnp.zeros(b_now, my_data.dtype)
+    for hop_no in [*range(view_out)]:
+        u1 = lax.dynamic_slice_in_dim(my_data, (front ^ hop_no) * o_now, o_now, axis=2)
+        if hop_no:
+            ledger = []
+            for s in tuple(range(view_out)):
+                ledger.append((s, s ^ hop_no))
+            u1 = jax.lax.ppermute(u1, axis_name=a_name, perm=ledger)
+        known = lax.dynamic_update_slice_in_dim(known, u1, (front ^ hop_no) * base_arr, axis=1)
+    return known
+
+
+clear_the_samples = functools.partial(turn_meshes, a_name="grid")
 
 
 def dft_pair(length, direction, rows=None, columns=None):
@@ -128,7 +153,7 @@
         table = forward if harmonic == 0 else forward * flip.reshape(2, 1, 1, 1)
         wave = ein("cxyz,cydk->dxkz", prod, table)
         wave = ein("dxkz,dzem->exkm", wave, forward)
-        wave = lax.all_to_all(wave, "grid", split_axis=2, concat_axis=1, tiled=True)
+        wave = clear_the_samples(wave)
         outs.append(ein("cxyz,cxdk->dkyz", wave, forward))
     return jnp.stack(outs, axis=0)[None]
 

time: 337 us -> 322 us (0.955)
  the two profiles are of different devices: /device:TPU:0 before, /device:TPU:8 now
where the time goes in v1:
time: 322 us; the launch traced here: 321 us
  waiting for transfers between devices  210 us (65%)
  starting transfers between devices  47 us (15%)
  local copies, waits for them, and re-layouts  32.1 us (10%)
  matrix products  25.5 us (8%)
  other arithmetic  5.63 us (2%)
    all_to_all x2, waiting for transfers between devices, on_device(): wave = lax.all_to_all(wave, 'grid', split_axis=1, concat_axis=2, tiled=True)  81.6 us
    ppermute x14, waiting for transfers between devices, turn_meshes(): u1 = jax.lax.ppermute(u1, axis_name=a_name, perm=ledger)  69 us
    ppermute x4, waiting for transfers between devices, swap(): return lax.ppermute(values, 'band', [(i, i ^ bit) for i in range(size)])  31.7 us
    dot_general x18, matrix products, ein(): return jnp.einsum(form, operand, table, precision=high)  25.5 us
    ppermute x14, starting transfers between devices, turn_meshes(): u1 = jax.lax.ppermute(u1, axis_name=a_name, perm=ledger)  20.9 us
    all_to_all x1, waiting for transfers between devices, hartree(): wave = lax.all_to_all(wave, axes, split_axis=2, concat_axis=1, tiled=True)  14.4 us
    all_to_all x1, waiting for transfers between devices, hartree(): wave = lax.all_to_all(wave, axes, split_axis=1, concat_axis=2, tiled=True)  13.3 us
    all_to_all x2, starting transfers between devices, on_device(): wave = lax.all_to_all(wave, 'grid', split_axis=1, concat_axis=2, tiled=True)  13.1 us
  transfers between devices with their start and end apart: 22, of which 17 were waited for; matrix products, arithmetic and copies ran while one was open for 6% of the time, Pallas kernels for 0%

profile of v1, /device:TPU:8, one launch (start us, length us, event | category | flops | bytes accessed | tf_op | source)
XLA Modules:
  0.0 320.9 jit_solution(5289235824450186333)
XLA Ops:
  0.0 4.0 %fusion.56 = (f32[1,1,2,128,16,128]{5,4,3,2,1,0:T(8,128)}, f32[1,1,2,128,16,128]{5,4,3,2,1,0:T(8,128)S(1)}) fusion(f32[1,2,2,128,16,128]{5,4,3,2,1,0:T(8,128)} %param.22), kind=kLoop, calls=%fused_computation.104 | loop fusion | bytes 8388608 | tf_op jit(solution)/shard_map/slice | solution.py:100
  8.3 6.3 %all-to-all-start.1 = ((f32[2,128,16,128]{3,2,0,1:T(8,128)}), f32[2,128,16,128]{3,2,0,1:T(8,128)}, u32[]{:S(2)}, u32[]{:S(2)}) async-start(f32[2,128,16,128]{3,2,0,1:T(8,128)} %copy.129), calls=%async_computation.1 | async-start | bytes 4194304 | tf_op jit(solution)/shard_map/all_to_all | solution.py:101
  14.5 3.2 fusion.33
  20.2 40.1 %all-to-all-done.1 = f32[2,128,16,128]{3,2,0,1:T(8,128)} async-done(((f32[2,128,16,128]{3,2,0,1:T(8,128)}), f32[2,128,16,128]{3,2,0,1:T(8,128)}, u32[]{:S(2)}, u32[]{:S(2)}) %all-to-all-start.1) | async-done | bytes 2097184 | tf_op jit(solution)/shard_map/all_to_all | solution.py:101
  60.3 6.8 %all-to-all-start = ((f32[2,128,16,128]{3,2,0,1:T(8,128)}), f32[2,128,16,128]{3,2,0,1:T(8,128)}, u32[]{:S(2)}, u32[]{:S(2)}) async-start(f32[2,128,16,128]{3,2,0,1:T(8,128)} %copy.121), calls=%async_computation | async-start | bytes 4194304 | tf_op jit(solution)/shard_map/all_to_all | solution.py:101
  67.5 3.2 copy.131
  70.6 41.5 %all-to-all-done = f32[2,128,16,128]{3,2,0,1:T(8,128)} async-done(((f32[2,128,16,128]{3,2,0,1:T(8,128)}), f32[2,128,16,128]{3,2,0,1:T(8,128)}, u32[]{:S(2)}, u32[]{:S(2)}) %all-to-all-start) | async-done | bytes 2097184 | tf_op jit(solution)/shard_map/all_to_all | solution.py:101
  128.6 12.8 %collective-permute-done.1 = f32[2,4,128,128]{2,3,0,1:T(8,128)} collective-permute-done((f32[2,4,128,128]{2,3,0,1:T(8,128)}, f32[2,4,128,128]{2,3,0,1:T(8,128)}, u32[]{:S(2)}, u32[]{:S(2)}) %collective-permute-start.1) | collective-permute-done | bytes 524320 | tf_op jit(solution)/shard_map/ppermute | solution.py:70
  144.6 6.4 %all-to-all-start.2 = ((f32[2,4,128,128]{3,0,1,2:T(2,128)}), f32[2,4,128,128]{3,0,1,2:T(2,128)}, u32[]{:S(2)}, u32[]{:S(2)}) async-start(f32[2,4,128,128]{3,0,1,2:T(2,128)} %copy.137), calls=%async_computation.2 | async-start | bytes 1048576 | tf_op jit(solution)/shard_map/all_to_all | solution.py:78
  151.9 14.4 %all-to-all-done.2 = f32[2,4,128,128]{3,0,1,2:T(2,128)} async-done(((f32[2,4,128,128]{3,0,1,2:T(2,128)}), f32[2,4,128,128]{3,0,1,2:T(2,128)}, u32[]{:S(2)}, u32[]{:S(2)}) %all-to-all-start.2) | async-done | bytes 524320 | tf_op jit(solution)/shard_map/all_to_all | solution.py:78
  170.4 4.5 %all-to-all-start.3 = ((f32[2,128,4,128]{3,2,0,1:T(4,128)}), f32[2,128,4,128]{3,2,0,1:T(4,128)}, u32[]{:S(2)}, u32[]{:S(2)}) async-start(f32[2,128,4,128]{3,2,0,1:T(4,128)} %copy.140), calls=%async_computation.3 | async-start | bytes 1048576 | tf_op jit(solution)/shard_map/all_to_all | solution.py:85
  176.8 13.3 %all-to-all-done.3 = f32[2,128,4,128]{3,2,0,1:T(4,128)} async-done(((f32[2,128,4,128]{3,2,0,1:T(4,128)}), f32[2,128,4,128]{3,2,0,1:T(4,128)}, u32[]{:S(2)}, u32[]{:S(2)}) %all-to-all-start.3) | async-done | bytes 524320 | tf_op jit(solution)/shard_map/all_to_all | solution.py:85
  194.9 13.5 %collective-permute-done.2 = f32[2,4,128,128]{2,3,0,1:T(8,128)} collective-permute-done((f32[2,4,128,128]{2,3,0,1:T(8,128)S(1)}, f32[2,4,128,128]{2,3,0,1:T(8,128)}, u32[]{:S(2)}, u32[]{:S(2)}) %collective-permute-start.2) | collective-permute-done | bytes 524320 | tf_op jit(solution)/shard_map/ppermute | solution.py:70
  228.0 7.6 %collective-permute-done.5 = f32[2,16,16,128]{3,2,0,1:T(8,128)S(1)} collective-permute-done((f32[2,16,16,128]{3,2,0,1:T(8,128)S(1)}, f32[2,16,16,128]{3,2,0,1:T(8,128)S(1)}, u32[]{:S(2)}, u32[]{:S(2)}) %collective-permute-start.5) | collective-permute-done | bytes 262176 | tf_op jit(solution)/shard_map/ppermute | solution.py:29
  240.2 4.0 %collective-permute-start.12 = (f32[2,16,16,128]{3,2,0,1:T(8,128)S(1)}, f32[2,16,16,128]{3,2,0,1:T(8,128)S(1)}, u32[]{:S(2)}, u32[]{:S(2)}) collective-permute-start(f32[2,16,16,128]{3,2,0,1:T(8,128)S(1)} %get-tuple-element.20), channel_id=1, source_target_pairs={{0,2},{1,3},{2,0},{3,1},{4,6},{5,7},{6,4},{7,5},{8,10},{9,11},{10,... | collective-permute-start | bytes 786440 | tf_op jit(solution)/shard_map/ppermute | solution.py:29
  244.4 12.8 %collective-permute-done.8 = f32[2,16,16,128]{3,2,0,1:T(8,128)S(1)} collective-permute-done((f32[2,16,16,128]{3,2,0,1:T(8,128)S(1)}, f32[2,16,16,128]{3,2,0,1:T(8,128)S(1)}, u32[]{:S(2)}, u32[]{:S(2)}) %collective-permute-start.8) | collective-permute-done | bytes 262176 | tf_op jit(solution)/shard_map/ppermute | solution.py:29
  257.3 4.2 %collective-permute-start.13 = (f32[2,16,16,128]{3,2,0,1:T(8,128)S(1)}, f32[2,16,16,128]{3,2,0,1:T(8,128)S(1)}, u32[]{:S(2)}, u32[]{:S(2)}) collective-permute-start(f32[2,16,16,128]{3,2,0,1:T(8,128)S(1)} %get-tuple-element.19), channel_id=1, source_target_pairs={{0,3},{1,2},{2,1},{3,0},{4,7},{5,6},{6,5},{7,4},{8,11},{9,10},{10,... | collective-permute-start | bytes 786440 | tf_op jit(solution)/shard_map/ppermute | solution.py:29
  264.8 12.2 %collective-permute-done.10 = f32[2,16,16,128]{3,2,0,1:T(8,128)S(1)} collective-permute-done((f32[2,16,16,128]{3,2,0,1:T(8,128)S(1)}, f32[2,16,16,128]{3,2,0,1:T(8,128)S(1)}, u32[]{:S(2)}, u32[]{:S(2)}) %collective-permute-start.10) | collective-permute-done | bytes 262176 | tf_op jit(solution)/shard_map/ppermute | solution.py:29
  278.4 3.9 %collective-permute-start.16 = (f32[2,16,16,128]{3,2,0,1:T(8,128)S(1)}, f32[2,16,16,128]{3,2,0,1:T(8,128)S(1)}, u32[]{:S(2)}, u32[]{:S(2)}) collective-permute-start(f32[2,16,16,128]{3,2,0,1:T(8,128)S(1)} %get-tuple-element.16), channel_id=1, source_target_pairs={{0,6},{1,7},{2,4},{3,5},{4,2},{5,3},{6,0},{7,1},{8,14},{9,15},{10,... | collective-permute-start | bytes 786440 | tf_op jit(solution)/shard_map/ppermute | solution.py:29
  283.2 13.5 %collective-permute-done.14 = f32[2,16,16,128]{3,2,0,1:T(8,128)S(1)} collective-permute-done((f32[2,16,16,128]{3,2,0,1:T(8,128)S(1)}, f32[2,16,16,128]{3,2,0,1:T(8,128)S(1)}, u32[]{:S(2)}, u32[]{:S(2)}) %collective-permute-start.14) | collective-permute-done | bytes 262176 | tf_op jit(solution)/shard_map/ppermute | solution.py:29
  296.9 5.5 %collective-permute-done.15 = f32[2,16,16,128]{3,2,0,1:T(8,128)S(1)} collective-permute-done((f32[2,16,16,128]{3,2,0,1:T(8,128)S(1)}, f32[2,16,16,128]{3,2,0,1:T(8,128)S(1)}, u32[]{:S(2)}, u32[]{:S(2)}) %collective-permute-start.15) | collective-permute-done | bytes 262176 | tf_op jit(solution)/shard_map/ppermute | solution.py:29
  302.5 7.1 %collective-permute-done.16 = f32[2,16,16,128]{3,2,0,1:T(8,128)S(1)} collective-permute-done((f32[2,16,16,128]{3,2,0,1:T(8,128)S(1)}, f32[2,16,16,128]{3,2,0,1:T(8,128)S(1)}, u32[]{:S(2)}, u32[]{:S(2)}) %collective-permute-start.16) | collective-permute-done | bytes 262176 | tf_op jit(solution)/shard_map/ppermute | solution.py:29
  309.8 4.8 %collective-permute-done.17 = f32[2,16,16,128]{3,2,0,1:T(8,128)S(1)} collective-permute-done((f32[2,16,16,128]{3,2,0,1:T(8,128)S(1)}, f32[2,16,16,128]{3,2,0,1:T(8,128)S(1)}, u32[]{:S(2)}, u32[]{:S(2)}) %collective-permute-start.17) | collective-permute-done | bytes 262176 | tf_op jit(solution)/shard_map/ppermute | solution.py:29
  316.5 4.4 %copy.167 = f32[1,2,2,128,16,128]{5,4,3,2,1,0:T(8,128)} copy(f32[1,2,2,128,16,128]{5,3,4,2,1,0:T(8,128)S(1)} %maximum_bitcast_fusion) | data formatting | bytes 8388608 | tf_op jit(solution)/shard_map/broadcast_in_dim | solution.py:158
  (108 shorter events, 70.3 us)
Async XLA Ops:
  0.0 174.9 %copy-start = (f32[16,128,128]{2,1,0:T(8,128)S(1)}, f32[16,128,128]{2,1,0:T(8,128)}, u32[]{:S(2)}) copy-start(f32[16,128,128]{2,1,0:T(8,128)} %param.23) | copy-start | bytes 3145732
  8.3 52.0 %all-to-all-start.1 = ((f32[2,128,16,128]{3,2,0,1:T(8,128)}), f32[2,128,16,128]{3,2,0,1:T(8,128)}, u32[]{:S(2)}, u32[]{:S(2)}) async-start(f32[2,128,16,128]{3,2,0,1:T(8,128)} %copy.129), calls=%async_computation.1 | async-start | bytes 4194304 | tf_op jit(solution)/shard_map/all_to_all | solution.py:101
  60.3 51.9 %all-to-all-start = ((f32[2,128,16,128]{3,2,0,1:T(8,128)}), f32[2,128,16,128]{3,2,0,1:T(8,128)}, u32[]{:S(2)}, u32[]{:S(2)}) async-start(f32[2,128,16,128]{3,2,0,1:T(8,128)} %copy.121), calls=%async_computation | async-start | bytes 4194304 | tf_op jit(solution)/shard_map/all_to_all | solution.py:101
  121.7 2.9 collective-permute-start
  127.0 14.3 %collective-permute-start.1 = (f32[2,4,128,128]{2,3,0,1:T(8,128)}, f32[2,4,128,128]{2,3,0,1:T(8,128)}, u32[]{:S(2)}, u32[]{:S(2)}) collective-permute-start(f32[2,4,128,128]{2,3,0,1:T(8,128)} %constant_dynamic-slice_fusion.1), channel_id=1, source_target_pairs={{0,16},{8,24},{16,0},{24,8},{1,17},{9,25},{17,1},{25,9},{2,18},{10... | collective-permute-start | bytes 1572872 | tf_op jit(solution)/shard_map/ppermute | solution.py:70
  144.6 21.7 %all-to-all-start.2 = ((f32[2,4,128,128]{3,0,1,2:T(2,128)}), f32[2,4,128,128]{3,0,1,2:T(2,128)}, u32[]{:S(2)}, u32[]{:S(2)}) async-start(f32[2,4,128,128]{3,0,1,2:T(2,128)} %copy.137), calls=%async_computation.2 | async-start | bytes 1048576 | tf_op jit(solution)/shard_map/all_to_all | solution.py:78
  170.4 19.7 %all-to-all-start.3 = ((f32[2,128,4,128]{3,2,0,1:T(4,128)}), f32[2,128,4,128]{3,2,0,1:T(4,128)}, u32[]{:S(2)}, u32[]{:S(2)}) async-start(f32[2,128,4,128]{3,2,0,1:T(4,128)} %copy.140), calls=%async_computation.3 | async-start | bytes 1048576 | tf_op jit(solution)/shard_map/all_to_all | solution.py:85
  194.3 14.1 %collective-permute-start.2 = (f32[2,4,128,128]{2,3,0,1:T(8,128)S(1)}, f32[2,4,128,128]{2,3,0,1:T(8,128)}, u32[]{:S(2)}, u32[]{:S(2)}) collective-permute-start(f32[2,4,128,128]{2,3,0,1:T(8,128)S(1)} %multiply_add_fusion), channel_id=1, source_target_pairs={{0,16},{8,24},{16,0},{24,8},{1,17},{9,25},{17,1},{25,9},{2,18},{10... | collective-permute-start | bytes 1572872 | tf_op jit(solution)/shard_map/ppermute | solution.py:70
  209.6 2.9 collective-permute-start.3
  218.1 9.1 %collective-permute-start.4 = (f32[2,16,16,128]{3,2,0,1:T(8,128)S(1)}, f32[2,16,16,128]{3,2,0,1:T(8,128)S(1)}, u32[]{:S(2)}, u32[]{:S(2)}) collective-permute-start(f32[2,16,16,128]{3,2,0,1:T(8,128)S(1)} %get-tuple-element.13), channel_id=1, source_target_pairs={{0,1},{1,0},{2,3},{3,2},{4,5},{5,4},{6,7},{7,6},{8,9},{9,8},{10,11... | collective-permute-start | bytes 786440 | tf_op jit(solution)/shard_map/ppermute | solution.py:29
  218.2 17.4 %collective-permute-start.5 = (f32[2,16,16,128]{3,2,0,1:T(8,128)S(1)}, f32[2,16,16,128]{3,2,0,1:T(8,128)S(1)}, u32[]{:S(2)}, u32[]{:S(2)}) collective-permute-start(f32[2,16,16,128]{3,2,0,1:T(8,128)S(1)} %get-tuple-element.12), channel_id=1, source_target_pairs={{0,2},{1,3},{2,0},{3,1},{4,6},{5,7},{6,4},{7,5},{8,10},{9,11},{10,... | collective-permute-start | bytes 786440 | tf_op jit(solution)/shard_map/ppermute | solution.py:29
  220.3 19.7 %collective-permute-start.6 = (f32[2,16,16,128]{3,2,0,1:T(8,128)S(1)}, f32[2,16,16,128]{3,2,0,1:T(8,128)S(1)}, u32[]{:S(2)}, u32[]{:S(2)}) collective-permute-start(f32[2,16,16,128]{3,2,0,1:T(8,128)S(1)} %get-tuple-element.11), channel_id=1, source_target_pairs={{0,3},{1,2},{2,1},{3,0},{4,7},{5,6},{6,5},{7,4},{8,11},{9,10},{10,... | collective-permute-start | bytes 786440 | tf_op jit(solution)/shard_map/ppermute | solution.py:29
  221.7 18.6 %collective-permute-start.7 = (f32[2,16,16,128]{3,2,0,1:T(8,128)S(1)}, f32[2,16,16,128]{3,2,0,1:T(8,128)S(1)}, u32[]{:S(2)}, u32[]{:S(2)}) collective-permute-start(f32[2,16,16,128]{3,2,0,1:T(8,128)S(1)} %get-tuple-element.10), channel_id=1, source_target_pairs={{0,4},{1,5},{2,6},{3,7},{4,0},{5,1},{6,2},{7,3},{8,12},{9,13},{10,... | collective-permute-start | bytes 786440 | tf_op jit(solution)/shard_map/ppermute | solution.py:29
  222.4 34.9 %collective-permute-start.8 = (f32[2,16,16,128]{3,2,0,1:T(8,128)S(1)}, f32[2,16,16,128]{3,2,0,1:T(8,128)S(1)}, u32[]{:S(2)}, u32[]{:S(2)}) collective-permute-start(f32[2,16,16,128]{3,2,0,1:T(8,128)S(1)} %get-tuple-element.9), channel_id=1, source_target_pairs={{0,5},{1,4},{2,7},{3,6},{4,1},{5,0},{6,3},{7,2},{8,13},{9,12},{10,... | collective-permute-start | bytes 786440 | tf_op jit(solution)/shard_map/ppermute | solution.py:29
  227.0 50.3 %copy-start.7 = (f32[2,128,2,128,1]{3,1,0,4,2:T(8,128)S(1)}, f32[2,128,2,128,1]{3,1,0,4,2:T(8,128)}, u32[]{:S(2)}) copy-start(f32[2,128,2,128,1]{3,1,0,4,2:T(8,128)} %constant.106) | copy-start | bytes 786436
  227.2 37.5 %collective-permute-start.9 = (f32[2,16,16,128]{3,2,0,1:T(8,128)S(1)}, f32[2,16,16,128]{3,2,0,1:T(8,128)S(1)}, u32[]{:S(2)}, u32[]{:S(2)}) collective-permute-start(f32[2,16,16,128]{3,2,0,1:T(8,128)S(1)} %get-tuple-element.8), channel_id=1, source_target_pairs={{0,6},{1,7},{2,4},{3,5},{4,2},{5,3},{6,0},{7,1},{8,14},{9,15},{10,... | collective-permute-start | bytes 786440 | tf_op jit(solution)/shard_map/ppermute | solution.py:29
  235.6 41.5 %collective-permute-start.10 = (f32[2,16,16,128]{3,2,0,1:T(8,128)S(1)}, f32[2,16,16,128]{3,2,0,1:T(8,128)S(1)}, u32[]{:S(2)}, u32[]{:S(2)}) collective-permute-start(f32[2,16,16,128]{3,2,0,1:T(8,128)S(1)} %get-tuple-element.7), channel_id=1, source_target_pairs={{0,7},{1,6},{2,5},{3,4},{4,3},{5,2},{6,1},{7,0},{8,15},{9,14},{10,... | collective-permute-start | bytes 786440 | tf_op jit(solution)/shard_map/ppermute | solution.py:29
  240.1 38.4 %collective-permute-start.11 = (f32[2,16,16,128]{3,2,0,1:T(8,128)S(1)}, f32[2,16,16,128]{3,2,0,1:T(8,128)S(1)}, u32[]{:S(2)}, u32[]{:S(2)}) collective-permute-start(f32[2,16,16,128]{3,2,0,1:T(8,128)S(1)} %get-tuple-element.21), channel_id=1, source_target_pairs={{0,1},{1,0},{2,3},{3,2},{4,5},{5,4},{6,7},{7,6},{8,9},{9,8},{10,11... | collective-permute-start | bytes 786440 | tf_op jit(solution)/shard_map/ppermute | solution.py:29
  240.2 42.3 %collective-permute-start.12 = (f32[2,16,16,128]{3,2,0,1:T(8,128)S(1)}, f32[2,16,16,128]{3,2,0,1:T(8,128)S(1)}, u32[]{:S(2)}, u32[]{:S(2)}) collective-permute-start(f32[2,16,16,128]{3,2,0,1:T(8,128)S(1)} %get-tuple-element.20), channel_id=1, source_target_pairs={{0,2},{1,3},{2,0},{3,1},{4,6},{5,7},{6,4},{7,5},{8,10},{9,11},{10,... | collective-permute-start | bytes 786440 | tf_op jit(solution)/shard_map/ppermute | solution.py:29
  257.3 25.8 %collective-permute-start.13 = (f32[2,16,16,128]{3,2,0,1:T(8,128)S(1)}, f32[2,16,16,128]{3,2,0,1:T(8,128)S(1)}, u32[]{:S(2)}, u32[]{:S(2)}) collective-permute-start(f32[2,16,16,128]{3,2,0,1:T(8,128)S(1)} %get-tuple-element.19), channel_id=1, source_target_pairs={{0,3},{1,2},{2,1},{3,0},{4,7},{5,6},{6,5},{7,4},{8,11},{9,10},{10,... | collective-permute-start | bytes 786440 | tf_op jit(solution)/shard_map/ppermute | solution.py:29
  264.7 32.1 %collective-permute-start.14 = (f32[2,16,16,128]{3,2,0,1:T(8,128)S(1)}, f32[2,16,16,128]{3,2,0,1:T(8,128)S(1)}, u32[]{:S(2)}, u32[]{:S(2)}) collective-permute-start(f32[2,16,16,128]{3,2,0,1:T(8,128)S(1)} %get-tuple-element.18), channel_id=1, source_target_pairs={{0,4},{1,5},{2,6},{3,7},{4,0},{5,1},{6,2},{7,3},{8,12},{9,13},{10,... | collective-permute-start | bytes 786440 | tf_op jit(solution)/shard_map/ppermute | solution.py:29
  277.1 25.3 %collective-permute-start.15 = (f32[2,16,16,128]{3,2,0,1:T(8,128)S(1)}, f32[2,16,16,128]{3,2,0,1:T(8,128)S(1)}, u32[]{:S(2)}, u32[]{:S(2)}) collective-permute-start(f32[2,16,16,128]{3,2,0,1:T(8,128)S(1)} %get-tuple-element.17), channel_id=1, source_target_pairs={{0,5},{1,4},{2,7},{3,6},{4,1},{5,0},{6,3},{7,2},{8,13},{9,12},{10,... | collective-permute-start | bytes 786440 | tf_op jit(solution)/shard_map/ppermute | solution.py:29
  278.4 31.2 %collective-permute-start.16 = (f32[2,16,16,128]{3,2,0,1:T(8,128)S(1)}, f32[2,16,16,128]{3,2,0,1:T(8,128)S(1)}, u32[]{:S(2)}, u32[]{:S(2)}) collective-permute-start(f32[2,16,16,128]{3,2,0,1:T(8,128)S(1)} %get-tuple-element.16), channel_id=1, source_target_pairs={{0,6},{1,7},{2,4},{3,5},{4,2},{5,3},{6,0},{7,1},{8,14},{9,15},{10,... | collective-permute-start | bytes 786440 | tf_op jit(solution)/shard_map/ppermute | solution.py:29
  282.5 32.2 %collective-permute-start.17 = (f32[2,16,16,128]{3,2,0,1:T(8,128)S(1)}, f32[2,16,16,128]{3,2,0,1:T(8,128)S(1)}, u32[]{:S(2)}, u32[]{:S(2)}) collective-permute-start(f32[2,16,16,128]{3,2,0,1:T(8,128)S(1)} %get-tuple-element.15), channel_id=1, source_target_pairs={{0,7},{1,6},{2,5},{3,4},{4,3},{5,2},{6,1},{7,0},{8,15},{9,14},{10,... | collective-permute-start | bytes 786440 | tf_op jit(solution)/shard_map/ppermute | solution.py:29
  (11 other events, 102.3 us)
